TPU v7x, 32 devices: a whole 2x2x4 slice. The times are simulated.
32 devices in a mesh: island: 8 (over y, x, core), fsdp: 4 (over z).
Axes of the slice: x: 2, y: 2, z: 4, core: 2. Of those that a mesh axis runs over, the one named last changes fastest.
Arguments:
- hidden: bfloat16 [4096, 4096], P(('island', 'fsdp')), may hold values from -6 to 6
- query_rows: bfloat16 [4096, 4096], P(('island', 'fsdp')), may hold values from -150 to 150
- key_rows: bfloat16 [4096, 512], P(('island', 'fsdp')), may hold values from -6 to 6
- targets: bfloat16 [4096, 4096], P(('island', 'fsdp')), may hold values from -6 to 6
- segment_ids: int32 [32, 128], P(('island', 'fsdp')), may hold values from 0 to 3, never falling along the last dimension, each value on 1 to 48 neighbouring positions
- first_moment: float32 [8, 4096, 512], P('island', 'fsdp'), may hold values from -0.0041432036 to 0.0041432036
- second_moment: float32 [8, 4096, 512], P('island', 'fsdp'), may hold values from 2.3841858e-07 to 3.8146973e-06
- anchor: float32 [4096, 512], P('fsdp', 'island'), may hold values from -6 to 6
- outer_momentum: float32 [4096, 512], P('fsdp', 'island'), may hold values from -0.3 to 0.3
- token_counts: int32 [8], P('island'), may hold values from 4096 to 12287
Outputs:
- new_anchor: float32 [4096, 512], P('fsdp', 'island')
- new_momentum: float32 [4096, 512], P('fsdp', 'island')
Inputs may be any that keep to these rules, and one draw needn't show every extreme that they name: `segment_ids`: each row is one sequence: document numbers from 0 that never fall, each document 1 to 48 tokens, one of exactly 48.
All inputs are finite; a program needn't handle non-finite values.
Results may differ from a plain program's by a relative error of at most 0.004.
Values may be sent and summed in bfloat16 or wider, within the bound.
A program may use at most 64 MiB of HBM per device.

v0:
```python
import math

import jax
import jax.numpy as jnp
from jax import lax
from jax.sharding import PartitionSpec as P

KVH = 4
QPK = 8
HD = 128


beta_one = 0.9
beta_two = 0.95
inner_rate = 0.05
decay = 0.1
epsilon = 1e-08
outer_rate = 0.7
outer_beta = 0.9


def attention_weights(query_rows, key_rows, segments):
    length = segments.shape[0]
    queries = query_rows.reshape(length, KVH, QPK, HD)
    keyed = key_rows.reshape(length, KVH, HD)
    scores = jnp.einsum("tgjd,sgd->gjts", queries, keyed, preferred_element_type=jnp.float32) * (
        1.0 / math.sqrt(HD)
    )
    place = jnp.arange(length)
    allowed = (place[None, :] <= place[:, None]) & (segments[:, None] == segments[None, :])
    scores = jnp.where(allowed[None, None], scores, -jnp.inf)
    highest = jnp.max(scores, axis=-1, keepdims=True)
    expo = jnp.exp(scores - highest)
    return (expo / jnp.sum(expo, axis=-1, keepdims=True)).astype(jnp.bfloat16)


def on_device(
    hidden,
    query_rows,
    key_rows,
    targets,
    segment_ids,
    first_moment,
    second_moment,
    anchor,
    outer_momentum,
    token_counts,
):
    rows = hidden.shape[0]
    width = key_rows.shape[1]
    group_rows = rows * lax.axis_size("fsdp")
    scale_in = 1.0 / math.sqrt(hidden.shape[1])
    attention = attention_weights(query_rows, key_rows, segment_ids[0])
    master = lax.all_gather(anchor, "island", axis=1, tiled=True)
    start_point = master
    block = master.shape[0]
    first = first_moment[0]
    second = second_moment[0]
    feature_rows = lax.all_to_all(hidden, "fsdp", split_axis=1, concat_axis=0, tiled=True)
    for inner_step in range(2):
        sent_rows = master.astype(jnp.bfloat16)
        add_piece = lax.all_gather(sent_rows, "fsdp", axis=0, tiled=True)
        count = add_piece.shape[0] // block
        columns = hidden.reshape(rows, count, block)
        blocks = jnp.einsum(
            "rks,ksw->krw",
            columns,
            add_piece.reshape(count, block, width),
            preferred_element_type=jnp.float32,
        )
        projected = jnp.sum(blocks.astype(jnp.bfloat16).astype(jnp.float32), axis=0)
        values = (projected * scale_in).astype(jnp.bfloat16)
        mixed = jnp.einsum(
            "gjts,sgd->tgjd",
            attention,
            values.reshape(rows, KVH, HD),
            preferred_element_type=jnp.float32,
        )
        error = (
            (mixed.reshape(rows, KVH * QPK * HD) - targets.astype(jnp.float32)) / group_rows
        ).astype(jnp.bfloat16)
        back = jnp.einsum(
            "gjts,tgjd->sgd",
            attention,
            error.reshape(rows, KVH, QPK, HD),
            preferred_element_type=jnp.float32,
        )
        value_grad = (back.reshape(rows, width) * scale_in).astype(jnp.bfloat16)
        grad = lax.dot_general(
            feature_rows,
            lax.all_gather(value_grad, "fsdp", axis=0, tiled=True),
            (((0,), (0,)), ((), ())),
            preferred_element_type=jnp.float32,
        )
        first = beta_one * first + (1.0 - beta_one) * grad
        second = beta_two * second + (1.0 - beta_two) * grad * grad
        master = master - inner_rate * (first / (jnp.sqrt(second) + epsilon) + decay * master)
    delta = start_point - master
    groups = lax.axis_size("island")
    own_count = token_counts[0].astype(jnp.float32)
    total_count = lax.psum(own_count, "island")
    received = lax.all_to_all(
        own_count / total_count * delta, "island", split_axis=1, concat_axis=0, tiled=True
    )
    average = jnp.sum(received.reshape(groups, block, anchor.shape[1]), axis=0)
    new_momentum = outer_beta * outer_momentum + average
    new_anchor = anchor - outer_rate * (average + outer_beta * new_momentum)
    return (new_anchor, new_momentum)


def solution(mesh):
    in_specs = (
        P(("island", "fsdp"), None),
        P(("island", "fsdp"), None),
        P(("island", "fsdp"), None),
        P(("island", "fsdp"), None),
        P(("island", "fsdp"), None),
        P("island", "fsdp", None),
        P("island", "fsdp", None),
        P("fsdp", "island"),
        P("fsdp", "island"),
        P("island"),
    )
    out_specs = (P("fsdp", "island"), P("fsdp", "island"))
    return jax.shard_map(
        on_device, mesh=mesh, in_specs=in_specs, out_specs=out_specs, check_vma=False
    )
```

profile of v0, /device:TPU:1, one launch (start us, length us, event | category | flops | bytes accessed | tf_op | source)
XLA Modules:
  0.0 330.4 jit_solution(5201902186861306081)
XLA Ops:
  7.2 0.7 all-gather.4.cloned.1.call-update
  8.0 32.4 %all-gather.4.cloned.1.call-done = f32[1024,512]{0,1:T(8,128)} async-done(((f32[1024,64]{0,1:T(8,128)}), f32[1024,512]{0,1:T(8,128)}) %all-gather.4.cloned.1.call-update) | async-done | bytes 2097168 | tf_op jit(solution)/shard_map/all_gather | solution.py:54
  40.3 2.8 convert_element_type.76
  43.1 1.3 copy.59
  44.4 4.5 %all-to-all-start = ((bf16[128,4,1024]{0,2,1:T(8,128)(2,1)}), bf16[128,4,1024]{0,2,1:T(8,128)(2,1)S(1)}, u32[]{:S(2)}, u32[]{:S(2)}) async-start(bf16[128,4,1024]{0,2,1:T(8,128)(2,1)} %bitcast.2), calls=%async_computation | async-start | bytes 2097152 | tf_op jit(solution)/shard_map/all_to_all | solution.py:59
  49.3 2.3 fusion.60
  51.6 1.9 divide_convert_fusion
  53.5 1.7 copy.67
  55.2 2.9 copy.58
  58.2 2.9 copy.69
  61.1 36.6 %all-to-all-done = bf16[128,4,1024]{0,2,1:T(8,128)(2,1)S(1)} async-done(((bf16[128,4,1024]{0,2,1:T(8,128)(2,1)}), bf16[128,4,1024]{0,2,1:T(8,128)(2,1)S(1)}, u32[]{:S(2)}, u32[]{:S(2)}) %all-to-all-start) | async-done | bytes 1048608 | tf_op jit(solution)/shard_map/all_to_all | solution.py:59
  97.7 1.3 copy.68
  99.0 44.1 %all-gather.6.cloned.1.call-done = bf16[4096,512]{0,1:T(8,128)(2,1)} async-done(((bf16[1024,512]{0,1:T(8,128)(2,1)}), bf16[4096,512]{0,1:T(8,128)(2,1)}) %all-gather.6.cloned.1.call-update) | async-done | bytes 4194320 | tf_op jit(solution)/shard_map/all_gather | solution.py:62
  143.1 6.5 %copy.60 = bf16[4096,512]{1,0:T(8,128)(2,1)} copy(bf16[4096,512]{0,1:T(8,128)(2,1)} %all-gather.6.cloned.1.call-done) | data formatting | bytes 8388608 | tf_op jit(solution)/shard_map/all_gather | solution.py:62
  149.6 3.3 %fusion.28 = f32[128,512]{1,0:T(8,128)S(1)} fusion(bf16[128,4,1024]{0,2,1:T(8,128)(2,1)} %bitcast.2, bf16[4,1024,512]{2,1,0:T(8,128)(2,1)} %bitcast.121), kind=kOutput, calls=%fused_computation.35 | convolution fusion | flops 537591808 | bytes 5505024 | tf_op jit(solution)/shard_map/rks,ksw->krw/dot_general | solution.py:65
  153.5 1.8 copy.66
  155.4 2.2 fusion.38
  157.8 1.0 copy-done.12
  158.8 0.5 fusion.35
  159.3 12.6 %all_gather.17 = bf16[512,512]{0,1:T(8,128)(2,1)S(1)} all-gather(bf16[128,512]{0,1:T(8,128)(2,1)S(1)} %bitcast.135), channel_id=1, replica_groups=mesh['island'=8,'fsdp'=4] {'fsdp'}, dimensions={0}, use_global_device_ids=true | all-gather | bytes 655360 | tf_op jit(solution)/shard_map/all_gather | solution.py:91
  171.9 3.6 %fusion.34 = (bf16[1024,512]{0,1:T(8,128)(2,1)}, f32[512,1024]{1,0:T(8,128)}) fusion(f32[1024,512]{0,1:T(8,128)S(1)} %copy-done.1, f32[1,1024,512]{1,2,0:T(8,128)S(1)} %copy-done.3, f32[1,1024,512]{1,2,0:T(8,128)S(1)} %copy-done.5, bf16[512,512]{0,1:T(8,128)(2,1)S(1)} %all_gather.17, bf16[512,1024]{1,0:T(8,128)(2,1)S(1)} %bitcast.127), kind=kOutput, calls=%fused_computation.41 | convolution fusion | flops 544210944 | bytes 11010048 | tf_op jit(solution)/shard_map/dot_general | solution.py:89
  176.1 15.6 %psum.7 = f32[]{:T(128)} all-reduce(f32[]{:T(128)} %bitcast), channel_id=1, replica_groups=mesh['island'=8,'fsdp'=4] {'island'}, use_global_device_ids=true, to_apply=%region_0.1 | all-reduce | flops 1 | bytes 8 | tf_op jit(solution)/shard_map/psum | solution.py:101
  192.4 64.1 %all-gather.8.cloned.1.call-done = bf16[4096,512]{0,1:T(8,128)(2,1)} async-done(((bf16[1024,512]{0,1:T(8,128)(2,1)}), bf16[4096,512]{0,1:T(8,128)(2,1)}) %all-gather.8.cloned.1.call-update) | async-done | bytes 4194320 | tf_op jit(solution)/shard_map/all_gather | solution.py:62
  256.5 3.8 %fusion.29 = f32[512,128]{1,0:T(8,128)S(1)} fusion(bf16[128,4,1024]{0,2,1:T(8,128)(2,1)} %bitcast.2, bf16[64,4,8,1024]{3,2,1,0:T(8,128)(2,1)} %bitcast.138), kind=kOutput, calls=%fused_computation.36 | convolution fusion | flops 537591808 | bytes 5505024 | tf_op jit(solution)/shard_map/rks,ksw->krw/dot_general | solution.py:65
  260.8 1.8 copy.73
  262.6 1.9 fusion.37
  264.8 1.0 copy-done.13
  266.3 12.4 %all_gather.19 = bf16[512,512]{0,1:T(8,128)(2,1)S(1)} all-gather(bf16[128,512]{0,1:T(8,128)(2,1)S(1)} %bitcast.134), channel_id=1, replica_groups=mesh['island'=8,'fsdp'=4] {'fsdp'}, dimensions={0}, use_global_device_ids=true | all-gather | bytes 655360 | tf_op jit(solution)/shard_map/all_gather | solution.py:91
  278.7 10.5 %fusion.19 = f32[1024,512]{0,1:T(8,128)S(1)} fusion(f32[1024,512]{0,1:T(8,128)S(1)} %copy-done.2, bf16[512,512]{0,1:T(8,128)(2,1)S(1)} %all_gather.19, bf16[512,1024]{1,0:T(8,128)(2,1)S(1)} %bitcast.128, f32[]{:T(128)S(6)} %div.23, f32[512,1024]{1,0:T(8,128)S(1)} %copy-done.17, f32[1,1024,512]{1,2,0:T(8,128)S(1)} %copy-done.4, f32[1,1024,512]{1,2,0:T(8,128)S(1)} %copy-done.6), kind=kOutput, calls=%fused_computation.29 | convolution fusion | flops 551550976 | bytes 12058628 | tf_op jit(solution)/shard_map/dot_general | solution.py:89
  289.2 32.7 %all_to_all.29 = f32[1024,8,64]{0,2,1:T(8,128)S(1)} all-to-all(f32[1024,8,64]{0,2,1:T(8,128)S(1)} %bitcast.125), channel_id=1, replica_groups=mesh['island'=8,'fsdp'=4] {'island'}, dimensions={1} | all-to-all | bytes 4194304 | tf_op jit(solution)/shard_map/all_to_all | solution.py:102
  322.1 0.8 copy-done.7
  323.0 0.9 multiply_subtract_fusion.1
  (50 shorter events, 2.7 us)
Async XLA Ops:
  7.2 33.2 %all-gather.4.cloned.1.call-start = ((), (), s32[]{:S(2)}) async-start(), calls=%async_computation.2 | async-start | bytes 2359296 | tf_op jit(solution)/shard_map/all_gather | solution.py:54
  7.9 35.2 %copy-start.8 = (bf16[128,4096]{1,0:T(8,128)(2,1)S(1)}, bf16[128,4096]{1,0:T(8,128)(2,1)}, u32[]{:S(2)}) copy-start(bf16[128,4096]{1,0:T(8,128)(2,1)} %param.10) | copy-start | bytes 3145732
  7.9 135.2 %all-gather.6.cloned.1.call-start = ((), (), s32[]{:S(2)}) async-start(), calls=%async_computation.3 | async-start | bytes 5242880 | tf_op jit(solution)/shard_map/all_gather | solution.py:62
  43.1 5.8 %copy-start.9 = (bf16[128,4096]{1,0:T(8,128)(2,1)S(1)}, bf16[128,4096]{1,0:T(8,128)(2,1)}, u32[]{:S(2)}) copy-start(bf16[128,4096]{1,0:T(8,128)(2,1)} %param.11) | copy-start | bytes 3145732
  44.4 4.7 %copy-start.15 = (bf16[128,512]{1,0:T(8,128)(2,1)S(1)}, bf16[128,512]{1,0:T(8,128)(2,1)}, u32[]{:S(2)}) copy-start(bf16[128,512]{1,0:T(8,128)(2,1)} %param.12) | copy-start | bytes 393220
  44.4 4.8 %copy-start.16 = (s32[1,128]{1,0:T(1,128)S(1)}, s32[1,128]{1,0:T(1,128)}, u32[]{:S(2)}) copy-start(s32[1,128]{1,0:T(1,128)} %param.14) | copy-start | bytes 1540
  44.4 53.3 %all-to-all-start = ((bf16[128,4,1024]{0,2,1:T(8,128)(2,1)}), bf16[128,4,1024]{0,2,1:T(8,128)(2,1)S(1)}, u32[]{:S(2)}, u32[]{:S(2)}) async-start(bf16[128,4,1024]{0,2,1:T(8,128)(2,1)} %bitcast.2), calls=%async_computation | async-start | bytes 2097152 | tf_op jit(solution)/shard_map/all_to_all | solution.py:59
  48.9 207.7 %all-gather.8.cloned.1.call-start = ((), (), s32[]{:S(2)}) async-start(), calls=%async_computation.4 | async-start | bytes 5242880 | tf_op jit(solution)/shard_map/all_gather | solution.py:62
  157.5 1.2 copy-start.12
  158.8 13.1 %copy-start.1 = (f32[1024,512]{0,1:T(8,128)S(1)}, f32[1024,512]{0,1:T(8,128)}, u32[]{:S(2)}) copy-start(f32[1024,512]{0,1:T(8,128)} %all-gather.4.cloned.1.call-done) | copy-start | bytes 6291460
  158.8 13.1 %copy-start.3 = (f32[1,1024,512]{1,2,0:T(8,128)S(1)}, f32[1,1024,512]{1,2,0:T(8,128)}, u32[]{:S(2)}) copy-start(f32[1,1024,512]{1,2,0:T(8,128)} %copy.58) | copy-start | bytes 6291460
  158.8 13.1 %copy-start.5 = (f32[1,1024,512]{1,2,0:T(8,128)S(1)}, f32[1,1024,512]{1,2,0:T(8,128)}, u32[]{:S(2)}) copy-start(f32[1,1024,512]{1,2,0:T(8,128)} %copy.69) | copy-start | bytes 6291460
  158.8 13.1 %copy-start.10 = (bf16[4,128,1024]{2,1,0:T(8,128)(2,1)S(1)}, bf16[4,128,1024]{2,1,0:T(8,128)(2,1)}, u32[]{:S(2)}) copy-start(bf16[4,128,1024]{2,1,0:T(8,128)(2,1)} %copy.68) | copy-start | bytes 3145732
  260.8 1.9 copy-start
  264.5 1.2 copy-start.13
  265.7 13.0 %copy-start.2 = (f32[1024,512]{0,1:T(8,128)S(1)}, f32[1024,512]{0,1:T(8,128)}, u32[]{:S(2)}) copy-start(f32[1024,512]{0,1:T(8,128)} %all-gather.4.cloned.1.call-done) | copy-start | bytes 6291460
  265.8 13.0 %copy-start.4 = (f32[1,1024,512]{1,2,0:T(8,128)S(1)}, f32[1,1024,512]{1,2,0:T(8,128)}, u32[]{:S(2)}) copy-start(f32[1,1024,512]{1,2,0:T(8,128)} %copy.58) | copy-start | bytes 6291460
  265.8 13.0 %copy-start.6 = (f32[1,1024,512]{1,2,0:T(8,128)S(1)}, f32[1,1024,512]{1,2,0:T(8,128)}, u32[]{:S(2)}) copy-start(f32[1,1024,512]{1,2,0:T(8,128)} %copy.69) | copy-start | bytes 6291460
  265.8 13.0 %copy-start.11 = (bf16[4,128,1024]{2,1,0:T(8,128)(2,1)S(1)}, bf16[4,128,1024]{2,1,0:T(8,128)(2,1)}, u32[]{:S(2)}) copy-start(bf16[4,128,1024]{2,1,0:T(8,128)(2,1)} %copy.68) | copy-start | bytes 3145732
  265.8 13.0 %copy-start.17 = (f32[512,1024]{1,0:T(8,128)S(1)}, f32[512,1024]{1,0:T(8,128)}, u32[]{:S(2)}) copy-start(f32[512,1024]{1,0:T(8,128)} %get-tuple-element.7) | copy-start | bytes 6291460
  322.0 1.0 copy-start.7
  322.0 1.0 copy-start.14
Sparse Core Ops, SparseCore 0:
  9.9 30.3 all-gather.3
  43.2 99.8 all-gather.5
  175.6 80.9 all-gather.7
where the time goes:
time: 332 us; the launch traced here: 330 us
  waiting for transfers between devices  178 us (54%)
  blocking collectives  73.4 us (22%)
  matrix products  25.2 us (8%)
  local copies, waits for them, and re-layouts  24.1 us (7%)
  between operations  15.3 us (5%)
  other arithmetic  9.88 us (3%)
  starting transfers between devices  4.53 us (1%)
    all_gather x2, waiting for transfers between devices, on_device(): add_piece = lax.all_gather(sent_rows, 'fsdp', axis=0, tiled=True)  108 us
    all_to_all x1, waiting for transfers between devices, on_device(): lax.all_to_all(hidden, 'fsdp', split_axis=1, concat_axis=0, tiled=True)  36.6 us
    all_to_all x1, blocking collectives, on_device(): lax.all_to_all(own_count / total_count * delta, 'island', split_axis=1, c...  32.7 us
    all_gather x1, waiting for transfers between devices, on_device(): master = lax.all_gather(anchor, 'island', axis=1, tiled=True)  32.4 us
    all_gather x2, blocking collectives, on_device(): lax.all_gather(value_grad, 'fsdp', axis=0, tiled=True)  25 us
    psum x1, blocking collectives, on_device(): total_count = lax.psum(own_count, 'island')  15.6 us
    dot_general x2, matrix products, on_device(): lax.dot_general(feature_rows, lax.all_gather(value_grad, 'fsdp', axis=0,...  14 us
    unnamed x42, local copies, waits for them, and re-layouts  10.7 us
  transfers between devices with their start and end apart: 4, of which 4 were waited for; matrix products, arithmetic and copies ran while one was open for 4% of the time, Pallas kernels for 0%

commit v1 on v0

--- a/solution.py
+++ b/solution.py
@@ -1,8 +1,11 @@
+import functools
 import math
 
 import jax
 import jax.numpy as jnp
 from jax import lax
+from jax.experimental import pallas as pl
+from jax.experimental.pallas import tpu as pltpu
 from jax.sharding import PartitionSpec as P
 
 KVH = 4
@@ -59,16 +62,11 @@
     feature_rows = lax.all_to_all(hidden, "fsdp", split_axis=1, concat_axis=0, tiled=True)
     for inner_step in range(2):
         sent_rows = master.astype(jnp.bfloat16)
-        add_piece = lax.all_gather(sent_rows, "fsdp", axis=0, tiled=True)
-        count = add_piece.shape[0] // block
-        columns = hidden.reshape(rows, count, block)
-        blocks = jnp.einsum(
-            "rks,ksw->krw",
-            columns,
-            add_piece.reshape(count, block, width),
-            preferred_element_type=jnp.float32,
-        )
-        projected = jnp.sum(blocks.astype(jnp.bfloat16).astype(jnp.float32), axis=0)
+        blocks = jnp.dot(feature_rows, sent_rows, preferred_element_type=jnp.float32)
+        pieces = lax.all_to_all(
+            blocks.astype(jnp.bfloat16), "fsdp", split_axis=0, concat_axis=0, tiled=True
+        )
+        projected = jnp.sum(pieces.reshape(-1, rows, width).astype(jnp.float32), axis=0)
         values = (projected * scale_in).astype(jnp.bfloat16)
         mixed = jnp.einsum(
             "gjts,sgd->tgjd",
@@ -106,6 +104,430 @@
     new_momentum = outer_beta * outer_momentum + average
     new_anchor = anchor - outer_rate * (average + outer_beta * new_momentum)
     return (new_anchor, new_momentum)
+
+
+MESH = pl.DeviceIdType.MESH
+BF = jnp.bfloat16
+F32 = jnp.float32
+
+
+def dot(left, right):
+    return jnp.dot(left, right, preferred_element_type=F32)
+
+
+def round_kernel(
+    ni,
+    nf,
+    hidden,
+    query,
+    keys,
+    targets,
+    segments,
+    first_in,
+    second_in,
+    anchor,
+    momentum,
+    counts,
+    new_anchor,
+    new_momentum,
+    q_buf,
+    t_buf,
+    first,
+    second,
+    feat,
+    feat_t,
+    att,
+    att_t,
+    weight,
+    master,
+    delta,
+    a_buf,
+    bv_send,
+    bv_recv,
+    vg_buf,
+    d_send,
+    d_recv,
+    local_sem,
+    h_send_sem,
+    h_recv_sem,
+    a_send_sem,
+    a_recv_sem,
+    b_send_sem,
+    b_recv_sem,
+    v_send_sem,
+    v_recv_sem,
+    d_send_sem,
+    d_recv_sem,
+):
+    me = lax.axis_index("fsdp")
+    island = lax.axis_index("island")
+    rows = feat.shape[1]
+    block = feat.shape[2]
+    half = block // 2
+    group_rows = rows * nf
+    scale_in = 1.0 / math.sqrt(hidden.shape[1])
+
+    def ahead(step):
+        return lax.rem(me + step, nf)
+
+    def behind(step):
+        return lax.rem(me + nf - step, nf)
+
+    def peer(step):
+        return lax.rem(island + step, ni)
+
+    loads = [
+        pltpu.make_async_copy(
+            hidden.at[:, pl.ds(pl.multiple_of(me * block, block), block)],
+            feat.at[0],
+            local_sem.at[0],
+        ),
+        pltpu.make_async_copy(query, q_buf, local_sem.at[1]),
+        pltpu.make_async_copy(targets, t_buf, local_sem.at[2]),
+        pltpu.make_async_copy(first_in, first, local_sem.at[3]),
+        pltpu.make_async_copy(second_in, second, local_sem.at[4]),
+    ]
+    for load in loads:
+        load.start()
+
+    barrier = pltpu.get_barrier_semaphore()
+    for step in range(1, nf):
+        pl.semaphore_signal(
+            barrier, inc=1, device_id=(island, ahead(step)), device_id_type=MESH
+        )
+    for step in range(1, ni):
+        pl.semaphore_signal(barrier, inc=1, device_id=(peer(step), me), device_id_type=MESH)
+
+    wide = anchor[...].astype(F32)
+    packed = jnp.concatenate([wide[:half], wide[half:]], axis=1)
+    a_buf[island, 0:half] = packed.astype(BF)
+    count = counts[0]
+    high = (count // 256).astype(F32)
+    low = (count % 256).astype(F32)
+    upper = lax.broadcasted_iota(jnp.int32, (16, 128), 0) < 8
+    a_buf[island, half : half + 16] = jnp.where(upper, high, low).astype(BF)
+
+    pl.semaphore_wait(barrier, ni + nf - 2)
+
+    def send_hidden(step):
+        return pltpu.make_async_remote_copy(
+            src_ref=hidden.at[:, pl.ds(pl.multiple_of(ahead(step) * block, block), block)],
+            dst_ref=feat.at[step],
+            send_sem=h_send_sem.at[step],
+            recv_sem=h_recv_sem.at[step],
+            device_id=(island, ahead(step)),
+            device_id_type=MESH,
+        )
+
+    def send_anchor(step):
+        return pltpu.make_async_remote_copy(
+            src_ref=a_buf.at[island],
+            dst_ref=a_buf.at[island],
+            send_sem=a_send_sem.at[step],
+            recv_sem=a_recv_sem.at[island],
+            device_id=(peer(step), me),
+            device_id_type=MESH,
+        )
+
+    def await_anchor(step):
+        owner = peer(step)
+        return pltpu.make_async_remote_copy(
+            src_ref=a_buf.at[owner],
+            dst_ref=a_buf.at[owner],
+            send_sem=a_send_sem.at[step],
+            recv_sem=a_recv_sem.at[owner],
+            device_id=(peer(step), me),
+            device_id_type=MESH,
+        )
+
+    def send_block(turn, head, step):
+        return pltpu.make_async_remote_copy(
+            src_ref=bv_send.at[turn, head, step],
+            dst_ref=bv_recv.at[turn, head, step],
+            send_sem=b_send_sem.at[turn, head, step],
+            recv_sem=b_recv_sem.at[turn, head, step],
+            device_id=(island, behind(step)),
+            device_id_type=MESH,
+        )
+
+    def send_grad(turn, head, step):
+        return pltpu.make_async_remote_copy(
+            src_ref=vg_buf.at[turn, head, 0:rows],
+            dst_ref=vg_buf.at[turn, head, step * rows : (step + 1) * rows],
+            send_sem=v_send_sem.at[turn, head, step],
+            recv_sem=v_recv_sem.at[turn, head, step],
+            device_id=(island, ahead(step)),
+            device_id_type=MESH,
+        )
+
+    def send_delta(owner):
+        return pltpu.make_async_remote_copy(
+            src_ref=d_send.at[owner],
+            dst_ref=d_recv.at[island],
+            send_sem=d_send_sem.at[owner],
+            recv_sem=d_recv_sem.at[island],
+            device_id=(owner, me),
+            device_id_type=MESH,
+        )
+
+    def await_delta(step):
+        owner = peer(step)
+        return pltpu.make_async_remote_copy(
+            src_ref=d_send.at[owner],
+            dst_ref=d_recv.at[owner],
+            send_sem=d_send_sem.at[owner],
+            recv_sem=d_recv_sem.at[owner],
+            device_id=(owner, me),
+            device_id_type=MESH,
+        )
+
+    near_first = [1, 3, 2] if nf == 4 else list(range(1, nf))
+    for step in near_first:
+        send_hidden(step).start()
+    for step in range(1, ni):
+        send_anchor(step).start()
+
+    loads[1].wait()
+    seg = jnp.broadcast_to(segments[...].astype(F32), (rows, rows))
+    place_t = lax.broadcasted_iota(jnp.int32, (rows, rows), 0)
+    place_s = lax.broadcasted_iota(jnp.int32, (rows, rows), 1)
+    allowed = (place_s <= place_t) & (seg == seg.T)
+
+    def attend(number, carry):
+        head = number // QPK
+        within = number % QPK
+        queries = q_buf[:, pl.ds(pl.multiple_of(number * HD, HD), HD)]
+        keyed = keys[:, pl.ds(pl.multiple_of(head * HD, HD), HD)]
+        scores = lax.dot_general(
+            queries, keyed, (((1,), (1,)), ((), ())), preferred_element_type=F32
+        ) * (1.0 / math.sqrt(HD))
+        scores = jnp.where(allowed, scores, -1e30)
+        expo = jnp.exp(scores - jnp.max(scores, axis=1, keepdims=True))
+        ratio = expo / jnp.sum(expo, axis=1, keepdims=True)
+        at = pl.ds(pl.multiple_of(within * rows, rows), rows)
+        att[head, at, :] = ratio.astype(BF)
+        att_t[head, :, at] = ratio.T.astype(BF)
+        return carry
+
+    lax.fori_loop(0, KVH * QPK, attend, 0, unroll=2)
+
+    for step in range(1, ni):
+        await_anchor(step).wait_recv()
+    left = lax.broadcasted_iota(jnp.int32, (half, 128), 1) < 64
+
+    def merge(head, carry):
+        even = a_buf[2 * head, 0:half].astype(F32)
+        odd = a_buf[2 * head + 1, 0:half].astype(F32)
+        top = jnp.where(left, even, pltpu.roll(odd, 64, 1))
+        bottom = jnp.where(left, pltpu.roll(even, 64, 1), odd)
+        master[head, 0:half] = top
+        master[head, half:block] = bottom
+        weight[head, 0:half] = top.astype(BF)
+        weight[head, half:block] = bottom.astype(BF)
+        return carry
+
+    lax.fori_loop(0, KVH, merge, 0)
+
+    for step in [0] + near_first:
+        if step == 0:
+            loads[0].wait()
+        else:
+            send_hidden(step).wait_recv()
+
+        def first_blocks(head, carry, step=step):
+            piece = dot(feat[step], weight[head]).astype(BF)
+            if step == 0:
+                bv_recv[0, head, 0] = piece
+            else:
+                bv_send[0, head, step] = piece
+                send_block(0, head, step).start()
+            return carry
+
+        lax.fori_loop(0, KVH, first_blocks, 0)
+    for step in range(nf):
+        feat_t[:, step * rows : (step + 1) * rows] = feat[step].T
+
+    def attention_turn(turn, head):
+        for step in range(1, nf):
+            send_block(turn, head, step).wait_recv()
+        projected = bv_recv[turn, head, 0].astype(F32)
+        for step in range(1, nf):
+            projected = projected + bv_recv[turn, head, step].astype(F32)
+        values = (projected * scale_in).astype(BF)
+        back = jnp.zeros((rows, HD), F32)
+        for within in range(QPK):
+            lot = slice(within * rows, (within + 1) * rows)
+            mixed = dot(att[head, lot, :], values)
+            aim = t_buf[:, pl.ds(pl.multiple_of((head * QPK + within) * HD, HD), HD)]
+            error = ((mixed - aim.astype(F32)) * (1.0 / group_rows)).astype(BF)
+            back = back + dot(att_t[head, :, lot], error)
+        vg_buf[turn, head, 0:rows] = (back * scale_in).astype(BF)
+        for step in near_first:
+            send_grad(turn, head, step).start()
+
+    def update_turn(turn, head):
+        for step in range(1, nf):
+            send_grad(turn, head, step).wait_recv()
+        lanes = pl.ds(pl.multiple_of(head * HD, HD), HD)
+        part = block // 4
+
+        def rows_part(index, carry):
+            at = pl.ds(pl.multiple_of(index * part, part), part)
+            grad = dot(feat_t[at, :], vg_buf[turn, head])
+            one = beta_one * first[0, at, lanes] + (1.0 - beta_one) * grad
+            two = beta_two * second[0, at, lanes] + (1.0 - beta_two) * grad * grad
+            now = master[head, at]
+            move = inner_rate * (one / (jnp.sqrt(two) + epsilon) + decay * now)
+            if turn == 0:
+                first[0, at, lanes] = one
+                second[0, at, lanes] = two
+                delta[head, at] = move
+                later = now - move
+                master[head, at] = later
+                weight[head, at] = later.astype(BF)
+            else:
+                delta[head, at] = (delta[head, at] + move) * count.astype(F32)
+            return carry
+
+        lax.fori_loop(0, 4, rows_part, 0)
+
+    def turn_one_attention(head, carry):
+        attention_turn(0, head)
+        return carry
+
+    def turn_one_update(head, carry):
+        update_turn(0, head)
+        for step in [1, 3, 2, 0] if nf == 4 else list(range(nf)):
+            piece = dot(feat[step], weight[head]).astype(BF)
+            if step == 0:
+                bv_recv[1, head, 0] = piece
+            else:
+                bv_send[1, head, step] = piece
+                send_block(1, head, step).start()
+        return carry
+
+    def turn_two_attention(head, carry):
+        attention_turn(1, head)
+        return carry
+
+    def turn_two_update(head, carry):
+        update_turn(1, head)
+        top = delta[head, 0:half]
+        bottom = delta[head, half:block]
+        d_send[2 * head] = jnp.where(left, top, pltpu.roll(bottom, 64, 1)).astype(BF)
+        d_send[2 * head + 1] = jnp.where(left, pltpu.roll(top, 64, 1), bottom).astype(BF)
+        for odd in range(2):
+            owner = 2 * head + odd
+
+            @pl.when(owner != island)
+            def _():
+                send_delta(owner).start()
+
+        return carry
+
+    loads[2].wait()
+    lax.fori_loop(0, KVH, turn_one_attention, 0)
+    loads[3].wait()
+    loads[4].wait()
+    lax.fori_loop(0, KVH, turn_one_update, 0)
+    lax.fori_loop(0, KVH, turn_two_attention, 0)
+    lax.fori_loop(0, KVH, turn_two_update, 0)
+
+    for step in range(1, ni):
+        await_delta(step).wait_recv()
+    total = d_send[island].astype(F32)
+    for step in range(1, ni):
+        total = total + d_recv[peer(step)].astype(F32)
+    tally = jnp.zeros((16, 128), F32)
+    for owner in range(ni):
+        tally = tally + a_buf[owner, half : half + 16].astype(F32)
+    whole = tally[0:1] * 256.0 + tally[8:9]
+    average = total / whole
+    pieces = (average[:, :64], pltpu.roll(average, 64, 1)[:, :64])
+    for place in range(2):
+        lot = slice(place * half, (place + 1) * half)
+        fresh = outer_beta * momentum[lot] + pieces[place]
+        new_momentum[lot] = fresh
+        new_anchor[lot] = anchor[lot] - outer_rate * (pieces[place] + outer_beta * fresh)
+
+    for step in range(1, nf):
+        send_hidden(step).wait_send()
+    for step in range(1, ni):
+        send_anchor(step).wait_send()
+        await_delta(step).wait_send()
+
+    def drain(number, carry):
+        turn = number // KVH
+        head = number % KVH
+        for step in range(1, nf):
+            send_block(turn, head, step).wait_send()
+            send_grad(turn, head, step).wait_send()
+        return carry
+
+    lax.fori_loop(0, 2 * KVH, drain, 0)
+
+
+def on_device_any(*args):
+    hidden, query, keys, _, _, first, _, anchor, _, _ = args
+    ni = lax.axis_size("island")
+    nf = lax.axis_size("fsdp")
+    rows = hidden.shape[0]
+    block, columns = anchor.shape
+    if (rows, columns, ni, block) != (HD, HD // 2, 2 * KVH, 8 * HD):
+        return on_device(*args)
+    vmem = pl.BlockSpec(memory_space=pltpu.VMEM)
+    anywhere = pl.BlockSpec(memory_space=pl.ANY)
+    dma = pltpu.SemaphoreType.DMA
+    return pl.pallas_call(
+        functools.partial(round_kernel, ni, nf),
+        out_shape=[jax.ShapeDtypeStruct(anchor.shape, F32)] * 2,
+        in_specs=[
+            anywhere,
+            anywhere,
+            vmem,
+            anywhere,
+            vmem,
+            anywhere,
+            anywhere,
+            vmem,
+            vmem,
+            pl.BlockSpec(memory_space=pltpu.SMEM),
+        ],
+        out_specs=[vmem, vmem],
+        scratch_shapes=[
+            pltpu.VMEM(query.shape, BF),
+            pltpu.VMEM(query.shape, BF),
+            pltpu.VMEM(first.shape, F32),
+            pltpu.VMEM(first.shape, F32),
+            pltpu.VMEM((nf, rows, block), BF),
+            pltpu.VMEM((block, nf * rows), BF),
+            pltpu.VMEM((KVH, QPK * rows, rows), BF),
+            pltpu.VMEM((KVH, rows, QPK * rows), BF),
+            pltpu.VMEM((KVH, block, HD), BF),
+            pltpu.VMEM((KVH, block, HD), F32),
+            pltpu.VMEM((KVH, block, HD), F32),
+            pltpu.VMEM((ni, block // 2 + 16, 128), BF),
+            pltpu.VMEM((2, KVH, nf, rows, HD), BF),
+            pltpu.VMEM((2, KVH, nf, rows, HD), BF),
+            pltpu.VMEM((2, KVH, nf * rows, HD), BF),
+            pltpu.VMEM((ni, block // 2, 128), BF),
+            pltpu.VMEM((ni, block // 2, 128), BF),
+            dma((5,)),
+            dma((nf,)),
+            dma((nf,)),
+            dma((ni,)),
+            dma((ni,)),
+            dma((2, KVH, nf)),
+            dma((2, KVH, nf)),
+            dma((2, KVH, nf)),
+            dma((2, KVH, nf)),
+            dma((ni,)),
+            dma((ni,)),
+        ],
+        compiler_params=pltpu.CompilerParams(
+            collective_id=0, has_side_effects=True, vmem_limit_bytes=44 * 2**20
+        ),
+    )(*args)
 
 
 def solution(mesh):
@@ -123,5 +545,5 @@
     )
     out_specs = (P("fsdp", "island"), P("fsdp", "island"))
     return jax.shard_map(
-        on_device, mesh=mesh, in_specs=in_specs, out_specs=out_specs, check_vma=False
+        on_device_any, mesh=mesh, in_specs=in_specs, out_specs=out_specs, check_vma=False
     )

time: 332 us -> 101 us (0.30)
  waiting for transfers between devices: 178 us -> 0 us
  Pallas kernels: 0 us -> 86.9 us
  blocking collectives: 73.4 us -> 0 us
  matrix products: 25.2 us -> 0 us
  between operations: 15.3 us -> 1.42 us
  local copies, waits for them, and re-layouts: 24.1 us -> 11.3 us
  other arithmetic: 9.88 us -> 0 us
  starting transfers between devices: 4.53 us -> 0 us
    all_gather x3 -> x0, waiting for transfers between devices: 141 us -> none  [the longest x2 108 us: on_device(): add_piece = lax.all_gather(sent_rows, 'fsdp', axis=0, tiled=True)]
    pallas_call x0 -> x1, Pallas kernels: none -> 86.9 us  [on_device_any(): pl.pallas_call(functools.partial(round_kernel, ni, nf), out_shape=[jax.Sh...]
    all_to_all x1 -> x0, waiting for transfers between devices: 36.6 us -> none  [on_device(): lax.all_to_all(hidden, 'fsdp', split_axis=1, concat_axis=0, tiled=True)]
    all_to_all x1 -> x0, blocking collectives: 32.7 us -> none  [on_device(): lax.all_to_all(own_count / total_count * delta, 'island', split_axis=1, c...]
    all_gather x2 -> x0, blocking collectives: 25 us -> none  [on_device(): lax.all_gather(value_grad, 'fsdp', axis=0, tiled=True)]
    dot_general x8 -> x0, matrix products: 22.9 us -> none  [the longest x2 14 us: on_device(): lax.dot_general(feature_rows, lax.all_gather(value_grad, 'fsdp', axis=0,...]
    psum x1 -> x0, blocking collectives: 15.6 us -> none  [on_device(): total_count = lax.psum(own_count, 'island')]
    all_gather x1 -> x0, local copies, waits for them, and re-layouts: 6.49 us -> none  [on_device(): add_piece = lax.all_gather(sent_rows, 'fsdp', axis=0, tiled=True)]
  transfers between devices with their start and end apart: 4 -> 0, of which waited for: 4 -> 0; matrix products, arithmetic and copies ran while one was open for 4% -> 0% of each run, Pallas kernels for 0% -> 0%
where the time goes in v1:
time: 101 us; the launch traced here: 99.6 us
  Pallas kernels  86.9 us (86%)
  local copies, waits for them, and re-layouts  11.3 us (11%)
  between operations  1.42 us (1%)
    pallas_call x1, Pallas kernels, on_device_any(): pl.pallas_call(functools.partial(round_kernel, ni, nf), out_shape=[jax.Sh...  86.9 us
    unnamed x16, local copies, waits for them, and re-layouts  9.48 us

profile of v1, /device:TPU:1, one launch (start us, length us, event | category | flops | bytes accessed | tf_op | source)
XLA Modules:
  0.0 99.6 jit_solution(14243285311273313424)
XLA Ops:
  0.6 0.0 copy-start.2
  1.4 1.1 %copy.12.anchor = f32[1024,64]{1,0:T(8,128)S(1)} copy(f32[1024,64]{0,1:T(8,128)} %param.17) | data formatting | bytes 524288 | tf_op args[7]
  2.5 1.1 %copy.13.momentum = f32[1024,64]{1,0:T(8,128)S(1)} copy(f32[1024,64]{0,1:T(8,128)} %param.18) | data formatting | bytes 524288 | tf_op args[8]
  3.7 0.0 copy-done.2
  3.7 0.0 copy-start
  3.7 1.6 %copy-done = f32[1,1024,512]{2,1,0:T(8,128)S(1)} copy-done((f32[1,1024,512]{2,1,0:T(8,128)S(1)}, f32[1,1024,512]{2,1,0:T(8,128)}, u32[]{:S(2)}) %copy-start) | copy-done | bytes 2097176
  5.3 0.0 copy-start.1
  5.3 1.6 %copy-done.1 = f32[1,1024,512]{2,1,0:T(8,128)S(1)} copy-done((f32[1,1024,512]{2,1,0:T(8,128)S(1)}, f32[1,1024,512]{2,1,0:T(8,128)}, u32[]{:S(2)}) %copy-start.1) | copy-done | bytes 2097176
  6.9 0.0 copy-start.3
  6.9 1.2 %copy-done.3 = bf16[128,4096]{1,0:T(8,128)(2,1)S(1)} copy-done((bf16[128,4096]{1,0:T(8,128)(2,1)S(1)}, bf16[128,4096]{1,0:T(8,128)(2,1)}, u32[]{:S(2)}) %copy-start.3) | copy-done | bytes 1048600
  8.1 0.0 copy-start.4
  8.1 1.2 %copy-done.4 = bf16[128,4096]{1,0:T(8,128)(2,1)S(1)} copy-done((bf16[128,4096]{1,0:T(8,128)(2,1)S(1)}, bf16[128,4096]{1,0:T(8,128)(2,1)}, u32[]{:S(2)}) %copy-start.4) | copy-done | bytes 1048600
  9.3 0.0 copy-start.5
  9.3 0.9 copy-done.5
  10.2 0.0 copy-start.6
  10.2 0.7 copy-done.6
  10.9 86.9 %shard_map.113 = (f32[1024,64]{1,0:T(8,128)S(1)}, f32[1024,64]{1,0:T(8,128)S(1)}) custom-call(bf16[128,4096]{1,0:T(8,128)(2,1)S(1)} %copy-done.2, bf16[128,4096]{1,0:T(8,128)(2,1)S(1)} %copy-done.3, bf16[128,512]{1,0:T(8,128)(2,1)S(1)} %copy-done.5, bf16[128,4096]{1,0:T(8,128)(2,1)S(1)} %copy-done.4, s32[1,128]{1,0:T(1,128)S(1)} %copy-done.6, ...), custom_call_target="tpu_custom_call" | custom-call | tf_op jit(solution)/shard_map/pallas_call | solution.py:481
  97.8 0.9 copy.14
  98.7 0.9 copy.15
Async XLA Ops:
  0.6 3.1 %copy-start.2 = (bf16[128,4096]{1,0:T(8,128)(2,1)S(1)}, bf16[128,4096]{1,0:T(8,128)(2,1)}, u32[]{:S(2)}) copy-start(bf16[128,4096]{1,0:T(8,128)(2,1)} %hidden.1) | copy-start | bytes 3145732
  3.7 1.6 %copy-start = (f32[1,1024,512]{2,1,0:T(8,128)S(1)}, f32[1,1024,512]{2,1,0:T(8,128)}, u32[]{:S(2)}) copy-start(f32[1,1024,512]{2,1,0:T(8,128)} %first_in.1) | copy-start | bytes 6291460
  5.3 1.6 %copy-start.1 = (f32[1,1024,512]{2,1,0:T(8,128)S(1)}, f32[1,1024,512]{2,1,0:T(8,128)}, u32[]{:S(2)}) copy-start(f32[1,1024,512]{2,1,0:T(8,128)} %second_in.1) | copy-start | bytes 6291460
  6.9 1.2 %copy-start.3 = (bf16[128,4096]{1,0:T(8,128)(2,1)S(1)}, bf16[128,4096]{1,0:T(8,128)(2,1)}, u32[]{:S(2)}) copy-start(bf16[128,4096]{1,0:T(8,128)(2,1)} %query.1) | copy-start | bytes 3145732
  8.1 1.2 %copy-start.4 = (bf16[128,4096]{1,0:T(8,128)(2,1)S(1)}, bf16[128,4096]{1,0:T(8,128)(2,1)}, u32[]{:S(2)}) copy-start(bf16[128,4096]{1,0:T(8,128)(2,1)} %targets.1) | copy-start | bytes 3145732
  9.3 0.9 copy-start.5
  10.2 0.7 copy-start.6

commit v2 on v1

--- a/solution.py
+++ b/solution.py
@@ -120,18 +120,21 @@
     nf,
     hidden,
     query,
-    keys,
+    keys_in,
     targets,
     segments,
     first_in,
     second_in,
-    anchor,
-    momentum,
+    anchor_in,
+    momentum_in,
     counts,
     new_anchor,
     new_momentum,
     q_buf,
     t_buf,
+    keys,
+    anchor,
+    momentum,
     first,
     second,
     feat,
@@ -142,6 +145,7 @@
     master,
     delta,
     a_buf,
+    c_buf,
     bv_send,
     bv_recv,
     vg_buf,
@@ -152,6 +156,8 @@
     h_recv_sem,
     a_send_sem,
     a_recv_sem,
+    c_send_sem,
+    c_recv_sem,
     b_send_sem,
     b_recv_sem,
     v_send_sem,
@@ -163,7 +169,7 @@
     island = lax.axis_index("island")
     rows = feat.shape[1]
     block = feat.shape[2]
-    half = block // 2
+    columns = anchor.shape[0]
     group_rows = rows * nf
     scale_in = 1.0 / math.sqrt(hidden.shape[1])
 
@@ -177,18 +183,21 @@
         return lax.rem(island + step, ni)
 
     loads = [
-        pltpu.make_async_copy(
-            hidden.at[:, pl.ds(pl.multiple_of(me * block, block), block)],
-            feat.at[0],
-            local_sem.at[0],
-        ),
+        pltpu.make_async_copy(anchor_in, anchor, local_sem.at[0]),
         pltpu.make_async_copy(query, q_buf, local_sem.at[1]),
         pltpu.make_async_copy(targets, t_buf, local_sem.at[2]),
         pltpu.make_async_copy(first_in, first, local_sem.at[3]),
         pltpu.make_async_copy(second_in, second, local_sem.at[4]),
+        pltpu.make_async_copy(keys_in, keys, local_sem.at[5]),
+        pltpu.make_async_copy(momentum_in, momentum, local_sem.at[6]),
+        pltpu.make_async_copy(
+            hidden.at[:, pl.ds(pl.multiple_of(me * block, block), block)],
+            feat.at[0],
+            local_sem.at[7],
+        ),
     ]
-    for load in loads:
-        load.start()
+    for number in (0, 5, 1):
+        loads[number].start()
 
     barrier = pltpu.get_barrier_semaphore()
     for step in range(1, nf):
@@ -197,15 +206,6 @@
         )
     for step in range(1, ni):
         pl.semaphore_signal(barrier, inc=1, device_id=(peer(step), me), device_id_type=MESH)
-
-    wide = anchor[...].astype(F32)
-    packed = jnp.concatenate([wide[:half], wide[half:]], axis=1)
-    a_buf[island, 0:half] = packed.astype(BF)
-    count = counts[0]
-    high = (count // 256).astype(F32)
-    low = (count % 256).astype(F32)
-    upper = lax.broadcasted_iota(jnp.int32, (16, 128), 0) < 8
-    a_buf[island, half : half + 16] = jnp.where(upper, high, low).astype(BF)
 
     pl.semaphore_wait(barrier, ni + nf - 2)
 
@@ -240,6 +240,30 @@
             device_id_type=MESH,
         )
 
+    def send_count(step):
+        return pltpu.make_async_remote_copy(
+            src_ref=c_buf.at[island],
+            dst_ref=c_buf.at[island],
+            send_sem=c_send_sem.at[step],
+            recv_sem=c_recv_sem.at[island],
+            device_id=(peer(step), me),
+            device_id_type=MESH,
+        )
+
+    def await_count(step):
+        owner = peer(step)
+        return pltpu.make_async_remote_copy(
+            src_ref=c_buf.at[owner],
+            dst_ref=c_buf.at[owner],
+            send_sem=c_send_sem.at[step],
+            recv_sem=c_recv_sem.at[owner],
+            device_id=(owner, me),
+            device_id_type=MESH,
+        )
+
+    def order(number):
+        return lax.rem(number + island // 2, KVH)
+
     def send_block(turn, head, step):
         return pltpu.make_async_remote_copy(
             src_ref=bv_send.at[turn, head, step],
@@ -284,9 +308,20 @@
     near_first = [1, 3, 2] if nf == 4 else list(range(1, nf))
     for step in near_first:
         send_hidden(step).start()
+    loads[0].wait()
+    a_buf[island] = anchor[...].astype(BF)
+    count = counts[0]
+    high = (count // 256).astype(F32)
+    low = (count % 256).astype(F32)
+    upper = lax.broadcasted_iota(jnp.int32, (16, 128), 0) < 8
+    c_buf[island] = jnp.where(upper, high, low).astype(BF)
     for step in range(1, ni):
         send_anchor(step).start()
-
+        send_count(step).start()
+    for number in (7, 2, 3, 4, 6):
+        loads[number].start()
+
+    loads[5].wait()
     loads[1].wait()
     seg = jnp.broadcast_to(segments[...].astype(F32), (rows, rows))
     place_t = lax.broadcasted_iota(jnp.int32, (rows, rows), 0)
@@ -313,28 +348,23 @@
 
     for step in range(1, ni):
         await_anchor(step).wait_recv()
-    left = lax.broadcasted_iota(jnp.int32, (half, 128), 1) < 64
 
     def merge(head, carry):
-        even = a_buf[2 * head, 0:half].astype(F32)
-        odd = a_buf[2 * head + 1, 0:half].astype(F32)
-        top = jnp.where(left, even, pltpu.roll(odd, 64, 1))
-        bottom = jnp.where(left, pltpu.roll(even, 64, 1), odd)
-        master[head, 0:half] = top
-        master[head, half:block] = bottom
-        weight[head, 0:half] = top.astype(BF)
-        weight[head, half:block] = bottom.astype(BF)
+        both = jnp.concatenate([a_buf[2 * head], a_buf[2 * head + 1]], axis=0).T
+        weight[head] = both
+        master[head] = both.astype(F32)
         return carry
 
     lax.fori_loop(0, KVH, merge, 0)
 
     for step in [0] + near_first:
         if step == 0:
-            loads[0].wait()
+            loads[7].wait()
         else:
             send_hidden(step).wait_recv()
 
-        def first_blocks(head, carry, step=step):
+        def first_blocks(number, carry, step=step):
+            head = order(number)
             piece = dot(feat[step], weight[head]).astype(BF)
             if step == 0:
                 bv_recv[0, head, 0] = piece
@@ -391,11 +421,13 @@
 
         lax.fori_loop(0, 4, rows_part, 0)
 
-    def turn_one_attention(head, carry):
+    def turn_one_attention(number, carry):
+        head = order(number)
         attention_turn(0, head)
         return carry
 
-    def turn_one_update(head, carry):
+    def turn_one_update(number, carry):
+        head = order(number)
         update_turn(0, head)
         for step in [1, 3, 2, 0] if nf == 4 else list(range(nf)):
             piece = dot(feat[step], weight[head]).astype(BF)
@@ -406,16 +438,17 @@
                 send_block(1, head, step).start()
         return carry
 
-    def turn_two_attention(head, carry):
+    def turn_two_attention(number, carry):
+        head = order(number)
         attention_turn(1, head)
         return carry
 
-    def turn_two_update(head, carry):
+    def turn_two_update(number, carry):
+        head = order(number)
         update_turn(1, head)
-        top = delta[head, 0:half]
-        bottom = delta[head, half:block]
-        d_send[2 * head] = jnp.where(left, top, pltpu.roll(bottom, 64, 1)).astype(BF)
-        d_send[2 * head + 1] = jnp.where(left, pltpu.roll(top, 64, 1), bottom).astype(BF)
+        turned = delta[head].astype(BF).T
+        d_send[2 * head] = turned[:columns]
+        d_send[2 * head + 1] = turned[columns:]
         for odd in range(2):
             owner = 2 * head + odd
 
@@ -438,22 +471,22 @@
     total = d_send[island].astype(F32)
     for step in range(1, ni):
         total = total + d_recv[peer(step)].astype(F32)
-    tally = jnp.zeros((16, 128), F32)
-    for owner in range(ni):
-        tally = tally + a_buf[owner, half : half + 16].astype(F32)
-    whole = tally[0:1] * 256.0 + tally[8:9]
+    tally = c_buf[island].astype(F32)
+    for step in range(1, ni):
+        await_count(step).wait_recv()
+        tally = tally + c_buf[peer(step)].astype(F32)
+    whole = tally[0:1, 0:1] * 256.0 + tally[8:9, 0:1]
     average = total / whole
-    pieces = (average[:, :64], pltpu.roll(average, 64, 1)[:, :64])
-    for place in range(2):
-        lot = slice(place * half, (place + 1) * half)
-        fresh = outer_beta * momentum[lot] + pieces[place]
-        new_momentum[lot] = fresh
-        new_anchor[lot] = anchor[lot] - outer_rate * (pieces[place] + outer_beta * fresh)
+    loads[6].wait()
+    fresh = outer_beta * momentum[...] + average
+    new_momentum[...] = fresh
+    new_anchor[...] = anchor[...] - outer_rate * (average + outer_beta * fresh)
 
     for step in range(1, nf):
         send_hidden(step).wait_send()
     for step in range(1, ni):
         send_anchor(step).wait_send()
+        send_count(step).wait_send()
         await_delta(step).wait_send()
 
     def drain(number, carry):
@@ -476,27 +509,23 @@
     if (rows, columns, ni, block) != (HD, HD // 2, 2 * KVH, 8 * HD):
         return on_device(*args)
     vmem = pl.BlockSpec(memory_space=pltpu.VMEM)
-    anywhere = pl.BlockSpec(memory_space=pl.ANY)
+    anywhere = pl.BlockSpec(memory_space=pltpu.HBM)
     dma = pltpu.SemaphoreType.DMA
-    return pl.pallas_call(
+    args = args[:7] + (anchor.T, args[8].T, args[9])
+    outs = pl.pallas_call(
         functools.partial(round_kernel, ni, nf),
-        out_shape=[jax.ShapeDtypeStruct(anchor.shape, F32)] * 2,
-        in_specs=[
-            anywhere,
-            anywhere,
-            vmem,
-            anywhere,
-            vmem,
-            anywhere,
-            anywhere,
-            vmem,
-            vmem,
-            pl.BlockSpec(memory_space=pltpu.SMEM),
-        ],
+        out_shape=[jax.ShapeDtypeStruct((columns, block), F32)] * 2,
+        in_specs=[anywhere] * 4
+        + [vmem]
+        + [anywhere] * 4
+        + [pl.BlockSpec(memory_space=pltpu.SMEM)],
         out_specs=[vmem, vmem],
         scratch_shapes=[
             pltpu.VMEM(query.shape, BF),
             pltpu.VMEM(query.shape, BF),
+            pltpu.VMEM(keys.shape, BF),
+            pltpu.VMEM((columns, block), F32),
+            pltpu.VMEM((columns, block), F32),
             pltpu.VMEM(first.shape, F32),
             pltpu.VMEM(first.shape, F32),
             pltpu.VMEM((nf, rows, block), BF),
@@ -506,15 +535,18 @@
             pltpu.VMEM((KVH, block, HD), BF),
             pltpu.VMEM((KVH, block, HD), F32),
             pltpu.VMEM((KVH, block, HD), F32),
-            pltpu.VMEM((ni, block // 2 + 16, 128), BF),
+            pltpu.VMEM((ni, columns, block), BF),
+            pltpu.VMEM((ni, 16, 128), BF),
             pltpu.VMEM((2, KVH, nf, rows, HD), BF),
             pltpu.VMEM((2, KVH, nf, rows, HD), BF),
             pltpu.VMEM((2, KVH, nf * rows, HD), BF),
-            pltpu.VMEM((ni, block // 2, 128), BF),
-            pltpu.VMEM((ni, block // 2, 128), BF),
-            dma((5,)),
+            pltpu.VMEM((ni, columns, block), BF),
+            pltpu.VMEM((ni, columns, block), BF),
+            dma((8,)),
             dma((nf,)),
             dma((nf,)),
+            dma((ni,)),
+            dma((ni,)),
             dma((ni,)),
             dma((ni,)),
             dma((2, KVH, nf)),
@@ -525,9 +557,10 @@
             dma((ni,)),
         ],
         compiler_params=pltpu.CompilerParams(
-            collective_id=0, has_side_effects=True, vmem_limit_bytes=44 * 2**20
+            collective_id=0, has_side_effects=True, vmem_limit_bytes=62 * 2**20
         ),
     )(*args)
+    return tuple(out.T for out in outs)
 
 
 def solution(mesh):

time: 101 us -> 93.1 us (0.922); the launches traced: 99.6 us -> 92.9 us
  local copies, waits for them, and re-layouts: 11.3 us -> 3.34 us
  Pallas kernels: 86.9 us -> 88.3 us
    unnamed x16 -> x2, local copies, waits for them, and re-layouts: 9.48 us -> 3.34 us
    pallas_call x2 -> x0, local copies, waits for them, and re-layouts: 1.77 us -> none  [on_device_any(): pl.pallas_call(functools.partial(round_kernel, ni, nf), out_shape=[jax.Sh...]
    pallas_call x1, Pallas kernels: 86.9 us -> 88.3 us  [on_device_any(): pl.pallas_call(functools.partial(round_kernel, ni, nf), out_shape=[jax.Sh...]
where the time goes in v2:
time: 93.1 us; the launch traced here: 92.9 us
  Pallas kernels  88.3 us (95%)
  local copies, waits for them, and re-layouts  3.34 us (4%)
  between operations  1.29 us (1%)
    pallas_call x1, Pallas kernels, on_device_any(): pl.pallas_call(functools.partial(round_kernel, ni, nf), out_shape=[jax.Sh...  88.3 us
    unnamed x2, local copies, waits for them, and re-layouts  3.34 us

profile of v2, /device:TPU:1, one launch (start us, length us, event | category | flops | bytes accessed | tf_op | source)
XLA Modules:
  0.0 92.9 jit_solution(15628936220978224310)
XLA Ops:
  1.3 88.3 %shard_map.113 = (f32[64,1024]{1,0:T(8,128)}, f32[64,1024]{1,0:T(8,128)}) custom-call(bf16[128,4096]{1,0:T(8,128)(2,1)} %hidden.1, bf16[128,4096]{1,0:T(8,128)(2,1)} %query.1, bf16[128,512]{1,0:T(8,128)(2,1)} %keys_in.1, bf16[128,4096]{1,0:T(8,128)(2,1)} %targets.1, s32[1,128]{1,0:T(1,128)} %segments.1, f32[1,1024,512]{2,1,0:T(8,128)} %first_in.1, ...), custom_call_target="tpu_custom_call" | custom-call | tf_op jit(solution)/shard_map/pallas_call | solution.py:515
  89.6 1.7 %copy.15 = f32[1024,64]{0,1:T(8,128)} copy(f32[1024,64]{0,1:T(8,128)} %bitcast.7) | data formatting | bytes 524288
  91.3 1.7 %copy.16 = f32[1024,64]{0,1:T(8,128)} copy(f32[1024,64]{0,1:T(8,128)} %bitcast.6) | data formatting | bytes 524288

commit v3 on v2

--- a/solution.py
+++ b/solution.py
@@ -429,8 +429,9 @@
     def turn_one_update(number, carry):
         head = order(number)
         update_turn(0, head)
-        for step in [1, 3, 2, 0] if nf == 4 else list(range(nf)):
-            piece = dot(feat[step], weight[head]).astype(BF)
+        whole_blocks = dot(feat[...].reshape(nf * rows, block), weight[head]).astype(BF)
+        for step in [2, 1, 3, 0] if nf == 4 else list(range(nf)):
+            piece = whole_blocks[step * rows : (step + 1) * rows]
             if step == 0:
                 bv_recv[1, head, 0] = piece
             else:

time: 93.1 us -> 93 us (level)
  no operation moved by 1% of the time
where the time goes in v3:
time: 93 us; the launch traced here: 92.8 us
  Pallas kernels  88.1 us (95%)
  local copies, waits for them, and re-layouts  3.34 us (4%)
  between operations  1.29 us (1%)
    pallas_call x1, Pallas kernels, on_device_any(): pl.pallas_call(functools.partial(round_kernel, ni, nf), out_shape=[jax.Sh...  88.1 us
    unnamed x2, local copies, waits for them, and re-layouts  3.34 us

profile of v3, /device:TPU:1, one launch (start us, length us, event | category | flops | bytes accessed | tf_op | source)
XLA Modules:
  0.0 92.8 jit_solution(10225581583300824490)
XLA Ops:
  1.3 88.1 %shard_map.113 = (f32[64,1024]{1,0:T(8,128)}, f32[64,1024]{1,0:T(8,128)}) custom-call(bf16[128,4096]{1,0:T(8,128)(2,1)} %hidden.1, bf16[128,4096]{1,0:T(8,128)(2,1)} %query.1, bf16[128,512]{1,0:T(8,128)(2,1)} %keys_in.1, bf16[128,4096]{1,0:T(8,128)(2,1)} %targets.1, s32[1,128]{1,0:T(1,128)} %segments.1, f32[1,1024,512]{2,1,0:T(8,128)} %first_in.1, ...), custom_call_target="tpu_custom_call" | custom-call | tf_op jit(solution)/shard_map/pallas_call | solution.py:516
  89.4 1.7 %copy.15 = f32[1024,64]{0,1:T(8,128)} copy(f32[1024,64]{0,1:T(8,128)} %bitcast.7) | data formatting | bytes 524288
  91.1 1.7 %copy.16 = f32[1024,64]{0,1:T(8,128)} copy(f32[1024,64]{0,1:T(8,128)} %bitcast.6) | data formatting | bytes 524288

commit v4 on v2

--- a/solution.py
+++ b/solution.py
@@ -462,9 +462,17 @@
     lax.fori_loop(0, KVH, turn_one_attention, 0)
     loads[3].wait()
     loads[4].wait()
-    lax.fori_loop(0, KVH, turn_one_update, 0)
-    lax.fori_loop(0, KVH, turn_two_attention, 0)
-    lax.fori_loop(0, KVH, turn_two_update, 0)
+    turn_one_update(0, 0)
+
+    def crossed(number, carry):
+        turn_one_update(number, carry)
+        turn_two_attention(number - 1, carry)
+        return carry
+
+    lax.fori_loop(1, KVH, crossed, 0)
+    turn_two_update(0, 0)
+    turn_two_attention(KVH - 1, 0)
+    lax.fori_loop(1, KVH, turn_two_update, 0)
 
     for step in range(1, ni):
         await_delta(step).wait_recv()

time: 93.1 us -> 91.7 us (0.985)
  Pallas kernels: 88.3 us -> 86.9 us
    pallas_call x1, Pallas kernels: 88.3 us -> 86.9 us  [on_device_any(): pl.pallas_call(functools.partial(round_kernel, ni, nf), out_shape=[jax.Sh...]
where the time goes in v4:
time: 91.7 us; the launch traced here: 91.5 us
  Pallas kernels  86.9 us (95%)
  local copies, waits for them, and re-layouts  3.34 us (4%)
  between operations  1.29 us (1%)
    pallas_call x1, Pallas kernels, on_device_any(): pl.pallas_call(functools.partial(round_kernel, ni, nf), out_shape=[jax.Sh...  86.9 us
    unnamed x2, local copies, waits for them, and re-layouts  3.34 us

profile of v4, /device:TPU:1, one launch (start us, length us, event | category | flops | bytes accessed | tf_op | source)
XLA Modules:
  0.0 91.5 jit_solution(1382260566076984549)
XLA Ops:
  1.3 86.9 %shard_map.113 = (f32[64,1024]{1,0:T(8,128)}, f32[64,1024]{1,0:T(8,128)}) custom-call(bf16[128,4096]{1,0:T(8,128)(2,1)} %hidden.1, bf16[128,4096]{1,0:T(8,128)(2,1)} %query.1, bf16[128,512]{1,0:T(8,128)(2,1)} %keys_in.1, bf16[128,4096]{1,0:T(8,128)(2,1)} %targets.1, s32[1,128]{1,0:T(1,128)} %segments.1, f32[1,1024,512]{2,1,0:T(8,128)} %first_in.1, ...), custom_call_target="tpu_custom_call" | custom-call | tf_op jit(solution)/shard_map/pallas_call | solution.py:523
  88.2 1.7 %copy.15 = f32[1024,64]{0,1:T(8,128)} copy(f32[1024,64]{0,1:T(8,128)} %bitcast.7) | data formatting | bytes 524288
  89.9 1.7 %copy.16 = f32[1024,64]{0,1:T(8,128)} copy(f32[1024,64]{0,1:T(8,128)} %bitcast.6) | data formatting | bytes 524288

commit v5 on v4

--- a/solution.py
+++ b/solution.py
@@ -306,7 +306,8 @@
         )
 
     near_first = [1, 3, 2] if nf == 4 else list(range(1, nf))
-    for step in near_first:
+    far_first = [2, 1, 3] if nf == 4 else near_first
+    for step in far_first:
         send_hidden(step).start()
     loads[0].wait()
     a_buf[island] = anchor[...].astype(BF)
@@ -392,7 +393,7 @@
             error = ((mixed - aim.astype(F32)) * (1.0 / group_rows)).astype(BF)
             back = back + dot(att_t[head, :, lot], error)
         vg_buf[turn, head, 0:rows] = (back * scale_in).astype(BF)
-        for step in near_first:
+        for step in far_first:
             send_grad(turn, head, step).start()
 
     def update_turn(turn, head):

time: 91.7 us -> 94.1 us (1.026); the launches traced: 91.5 us -> 92.8 us
  Pallas kernels: 86.9 us -> 88.2 us
    pallas_call x1, Pallas kernels: 86.9 us -> 88.2 us  [on_device_any(): pl.pallas_call(functools.partial(round_kernel, ni, nf), out_shape=[jax.Sh...]
where the time goes in v5:
time: 94.1 us; the launch traced here: 92.8 us
  Pallas kernels  88.2 us (94%)
  local copies, waits for them, and re-layouts  3.34 us (4%)
  between operations  1.29 us (1%)
    pallas_call x1, Pallas kernels, on_device_any(): pl.pallas_call(functools.partial(round_kernel, ni, nf), out_shape=[jax.Sh...  88.2 us
    unnamed x2, local copies, waits for them, and re-layouts  3.34 us

profile of v5, /device:TPU:1, one launch (start us, length us, event | category | flops | bytes accessed | tf_op | source)
XLA Modules:
  0.0 92.8 jit_solution(6900938835850316104)
XLA Ops:
  1.3 88.2 %shard_map.113 = (f32[64,1024]{1,0:T(8,128)}, f32[64,1024]{1,0:T(8,128)}) custom-call(bf16[128,4096]{1,0:T(8,128)(2,1)} %hidden.1, bf16[128,4096]{1,0:T(8,128)(2,1)} %query.1, bf16[128,512]{1,0:T(8,128)(2,1)} %keys_in.1, bf16[128,4096]{1,0:T(8,128)(2,1)} %targets.1, s32[1,128]{1,0:T(1,128)} %segments.1, f32[1,1024,512]{2,1,0:T(8,128)} %first_in.1, ...), custom_call_target="tpu_custom_call" | custom-call | tf_op jit(solution)/shard_map/pallas_call | solution.py:524
  89.5 1.7 %copy.15 = f32[1024,64]{0,1:T(8,128)} copy(f32[1024,64]{0,1:T(8,128)} %bitcast.7) | data formatting | bytes 524288
  91.2 1.7 %copy.16 = f32[1024,64]{0,1:T(8,128)} copy(f32[1024,64]{0,1:T(8,128)} %bitcast.6) | data formatting | bytes 524288
